TPU v7x, 256 devices: a whole 4x4x8 slice. The times are simulated.
256 devices in a mesh: tm: 16 (over z_hi, y, core), space: 16 (over x, z_lo).
Axes of the slice: x: 4, y: 4, z: 8 (z_hi: 2, z_lo: 4; z = z_hi * 4 + z_lo), core: 2. Of those that a mesh axis runs over, the one named last changes fastest.
Arguments:
- initial: float32 [64, 4096], P(None, 'space'), may hold values from -6 to 6
- guess: float32 [16, 64, 4096], P('tm', None, 'space'), may hold values from -6 to 6
- forcing: float32 [64, 64, 4096], P('tm', None, 'space'), may hold values from -1.8 to 1.8
- fine_inverse: float32 [64, 64, 4096], P(None, None, 'space'), as said below
- coarse_inverse: float32 [64, 64, 4096], P(None, None, 'space'), as said below
- neighbour: int32 [6, 4096], P(None, 'space'), may hold values from 0 to 511, as said below
- send_low: int32 [2048], P('space'), may hold values from 0 to 255, as said below
- send_high: int32 [2048], P('space'), may hold values from 0 to 255, as said below
- trace_map: float32 [6, 32, 64], replicated, may hold values from -0.75 to 0.75
- lift_map: float32 [6, 64, 32], replicated, may hold values from -0.09 to 0.09
Outputs:
- solution: float32 [64, 64, 4096], P('tm', None, 'space')
Inputs may be any that keep to these rules, and one draw needn't show every extreme that they name: `neighbour`: each block's elements form 2 x 8 x 16 hexahedra, periodic along y and z inside the block, numbered in a random order. Along x, an element's face to another block names slot 256 + k or 384 + k, where k is the face's position in the neighbouring block's boundary map; every other face names a local id. `send_low`: each block's 128 entries are its elements of the lowest x layer, face k of block s meeting face k of block s - 1's upper map. `send_high`: each block's 128 entries are its elements of the highest x layer, face k of block s meeting face k of block s + 1's lower map. `fine_inverse`: each block is a dominant diagonal plus a skew-symmetric full part. `coarse_inverse`: each block is a dominant diagonal plus a skew-symmetric full part.
All inputs are finite; a program needn't handle non-finite values.
Results may differ from a plain program's by a relative error of at most 0.00014.
Values sent between devices are 32-bit elements; how exact they have to be, the bound alone decides.
No kernel may reach another device: no remote copies, remote signals or barrier semaphores. Data moves between devices by JAX's collectives and lax.ppermute only.
A program may use at most 64 MiB of HBM per device.

v0:
```python
import jax
import jax.numpy as jnp
from jax import lax
from jax.sharding import PartitionSpec as P

SWEEPS = 2
STEPS_IN = 4


HIGH = lax.Precision.HIGHEST


def padded_2(array, sides, width):
    for axis, dim in sides:
        count, length = (lax.axis_size(axis), array.shape[dim])
        up = [(i, (i + 1) % count) for i in range(count - 1)]
        down = [(j, i) for i, j in up]
        last = lax.slice_in_dim(array, length - width, length, axis=dim)
        leading = lax.slice_in_dim(array, 0, width, axis=dim)
        before = lax.ppermute(last, axis, up)
        after = lax.ppermute(leading, axis, down)
        array = jnp.concatenate([before, array, after], axis=dim)
    return array


def shifted(block, axis, distance):
    devices = range(lax.axis_size(axis))
    route = [(i - distance, i) for i in devices if i - distance in devices]
    return lax.ppermute(block, axis, route)


def trace_all(current, trace_map):
    return jnp.einsum("dtj,je->dte", trace_map, current, precision=HIGH)


def outgoing(traces, send_low, send_high):
    return jnp.stack(
        [jnp.take(traces[0], send_low, axis=1), jnp.take(traces[1], send_high, axis=1)]
    )


def couple(traces, from_below, from_above, neighbour, lift_map):
    gathered = []
    for face_index in range(6):
        lookup = jnp.concatenate([traces[face_index ^ 1], from_below, from_above], axis=1)
        gathered.append(jnp.take(lookup, neighbour[face_index], axis=1))
    return jnp.einsum("fit,fte->ie", lift_map, jnp.stack(gathered), precision=HIGH)


def jacobi(right_side, inverse, coupled):
    return jnp.einsum("ije,je->ie", inverse, right_side - coupled, precision=HIGH)


def local(
    initial,
    guess,
    forcing,
    fine_inverse,
    coarse_inverse,
    neighbour,
    send_low,
    send_high,
    trace_map,
    lift_map,
):
    slab_index = lax.axis_index("tm")
    slab_count = lax.axis_size("tm")

    def sweep(current, right_side, inverse):
        traces = trace_all(current, trace_map)
        leaving = outgoing(traces, send_low, send_high)
        padded = padded_2(leaving, (("space", 0),), 1)
        coupled = couple(traces, padded[0], padded[3], neighbour, lift_map)
        return jacobi(right_side, inverse, coupled)

    def propagate(current, right_side, inverse):
        updated = current
        for sweep_index in range(SWEEPS):
            updated = sweep(updated, right_side, inverse)
        return updated

    def advance(current, forcing_now):
        return propagate(current, current + forcing_now, fine_inverse)

    def previous(end_state):
        moved = shifted(end_state, "tm", 1)
        return jnp.where(slab_index == 0, initial, moved)

    def relax(anchor):
        points = []
        current = anchor
        for inner_step in range(STEPS_IN - 1):
            current = advance(current, forcing[inner_step])
            points.append(current)
        return points

    first_pass = relax(previous(guess[0]))
    residual = advance(first_pass[-1], forcing[STEPS_IN - 1]) - guess[0]

    def relay_turn(turn_index, carried):
        incoming = shifted(carried, "tm", 1)
        return propagate(incoming, incoming, coarse_inverse) + residual

    correction = lax.fori_loop(1, slab_count, relay_turn, residual)
    final_end = guess[0] + correction
    last_pass = relax(previous(final_end))
    return jnp.stack(last_pass + [final_end])


def solution(mesh):
    in_specs = (
        P(None, "space"),
        P("tm", None, "space"),
        P("tm", None, "space"),
        P(None, None, "space"),
        P(None, None, "space"),
        P(None, "space"),
        P("space"),
        P("space"),
        P(),
        P(),
    )
    out_specs = P("tm", None, "space")
    return jax.shard_map(local, mesh=mesh, in_specs=in_specs, out_specs=out_specs, check_vma=False)
```

profile of v0, /device:TPU:134, one launch (start us, length us, event | category | flops | bytes accessed | tf_op | source)
XLA Modules:
  0.0 1162.3 jit_solution(10118020105302337288)
XLA Ops:
  5.7 6.1 collective-permute-done.5
  21.6 5.5 collective-permute-done.6
  110.1 4.4 collective-permute-done.14
  189.6 829.2 %while.10 = (s32[]{:T(128)}, f32[64,256]{1,0:T(8,128)S(1)}, f32[6,32,64]{2,1,0:T(8,128)S(1)}, s32[128]{0:T(128)S(1)}, s32[128]{0:T(128)S(1)}, /*index=5*/s32[6,2...) while((s32[]{:T(128)}, f32[64,256]{1,0:T(8,128)S(1)}, ...), condition=%wide.region_1.4_spmd, body=%wide.region_0.0_spmd.sunk | while | flops 155737856 | bytes 18247212 | solution.py:104
  191.8 9.4 collective-permute-done
  230.9 4.4 collective-permute-done.4
  247.1 9.4 collective-permute-done
  286.2 4.4 collective-permute-done.4
  302.4 9.4 collective-permute-done
  341.5 4.4 collective-permute-done.4
  357.7 9.4 collective-permute-done
  396.8 4.4 collective-permute-done.4
  413.0 9.4 collective-permute-done
  452.0 4.4 collective-permute-done.4
  468.2 9.4 collective-permute-done
  507.3 4.4 collective-permute-done.4
  523.5 9.4 collective-permute-done
  562.6 4.4 collective-permute-done.4
  578.8 9.4 collective-permute-done
  617.9 4.4 collective-permute-done.4
  634.1 9.4 collective-permute-done
  689.3 9.4 collective-permute-done
  728.4 4.4 collective-permute-done.4
  744.6 9.4 collective-permute-done
  799.9 9.4 collective-permute-done
  839.0 4.4 collective-permute-done.4
  855.2 9.4 collective-permute-done
  910.4 9.4 collective-permute-done
  949.5 4.4 collective-permute-done.4
  965.7 9.4 collective-permute-done
  1020.7 9.7 collective-permute-done.22
  1060.1 4.4 collective-permute-done.25
  (2444 shorter events, 930.5 us)
Async XLA Ops:
  0.0 11.8 %collective-permute-start.5 = (f32[64,256]{1,0:T(8,128)}, f32[64,256]{1,0:T(8,128)S(1)}, u32[]{:S(2)}, u32[]{:S(2)}) collective-permute-start(f32[64,256]{1,0:T(8,128)} %bitcast.1237), channel_id=1, source_target_pairs={{0,16},{16,32},{32,48},{48,64},{64,80},{80,96},{96,112},{112,128},... | collective-permute-start | bytes 196616 | tf_op jit(solution)/shard_map/ppermute | solution.py:29
  18.8 8.3 collective-permute-start.6
  40.6 8.3 collective-permute-start.8
  62.5 8.3 collective-permute-start.10
  84.3 8.3 collective-permute-start.12
  106.1 8.3 collective-permute-start.14
  127.9 8.3 collective-permute-start.16
  149.8 8.3 collective-permute-start.18
  171.6 8.3 collective-permute-start.20
  189.6 11.6 %collective-permute-start = (f32[64,256]{1,0:T(8,128)S(1)}, f32[64,256]{1,0:T(8,128)S(1)}, u32[]{:S(2)}, u32[]{:S(2)}) collective-permute-start(f32[64,256]{1,0:T(8,128)S(1)} %get-tuple-element.435), channel_id=1, source_target_pairs={{0,16},{16,32},{32,48},{48,64},{64,80},{80,96},{96,112},{112,128},... | collective-permute-start | bytes 196616 | tf_op jit(solution)/shard_map/while/body/eval_jaxpr/ppermute | solution.py:29
  205.2 8.3 collective-permute-start.2
  227.0 8.3 collective-permute-start.4
  244.9 11.6 collective-permute-start
  260.4 8.3 collective-permute-start.2
  282.2 8.3 collective-permute-start.4
  300.2 11.6 collective-permute-start
  315.7 8.3 collective-permute-start.2
  337.5 8.3 collective-permute-start.4
  355.5 11.6 collective-permute-start
  371.0 8.3 collective-permute-start.2
  410.8 11.6 collective-permute-start
  466.0 11.6 collective-permute-start
  521.3 11.6 collective-permute-start
  576.6 11.6 collective-permute-start
  631.9 11.6 collective-permute-start
  687.1 11.6 collective-permute-start
  742.4 11.6 collective-permute-start
  797.7 11.6 collective-permute-start
  853.0 11.6 collective-permute-start
  908.2 11.6 collective-permute-start
  963.5 11.6 collective-permute-start
  1018.8 11.6 collective-permute-start.22
  (81 other events, 1450.0 us)
where the time goes:
time: 1170 us; the launch traced here: 1160 us
  waiting for transfers between devices  350 us (30%)
  local copies, waits for them, and re-layouts  320 us (27%)
  starting transfers between devices  292 us (25%)
  other arithmetic  159 us (14%)
  matrix products  29.7 us (3%)
    gather x264, local copies, waits for them, and re-layouts, couple(): gathered.append(jnp.take(lookup, neighbour[face_index], axis=1))  194 us
    ppermute x44, waiting for transfers between devices, padded_2(): before = lax.ppermute(last, axis, up)  193 us
    ppermute x44, starting transfers between devices, padded_2(): before = lax.ppermute(last, axis, up)  172 us
    ppermute x17, waiting for transfers between devices, shifted(): return lax.ppermute(block, axis, route)  157 us
    dot_general x44, other arithmetic, jacobi(): jnp.einsum('ije,je->ie', inverse, right_side - coupled, precision=HIGH)  125 us
    ppermute x44, starting transfers between devices, padded_2(): after = lax.ppermute(leading, axis, down)  87.1 us
    concatenate x264, local copies, waits for them, and re-layouts, couple(): jnp.concatenate([traces[face_index ^ 1], from_below, from_above], axis=1)  34.6 us
    ppermute x17, starting transfers between devices, shifted(): return lax.ppermute(block, axis, route)  32.6 us
  transfers between devices with their start and end apart: 105, of which 61 were waited for; matrix products, arithmetic and copies ran while one was open for 4% of the time, Pallas kernels for 0%

commit v1 on v0

v1 whole, which is shorter than its diff:
```python
import functools

import jax
import jax.numpy as jnp
from jax import lax
from jax.experimental import pallas as pl
from jax.experimental.pallas import tpu as pltpu
from jax.sharding import PartitionSpec as P

DOFS = 64
TRACE = 32
LANES = 128
ELEMS = 256
F32 = jnp.float32
BF16 = jnp.bfloat16

VMEM = pl.BlockSpec(memory_space=pltpu.VMEM)
SMEM = pl.BlockSpec(memory_space=pltpu.SMEM)


def halves(x):
    high = x.astype(BF16)
    return high, (x - high.astype(F32)).astype(BF16)


def dot(a, b):
    return jnp.dot(a, b, preferred_element_type=F32)


def dot3(weights, x):
    high, low = halves(x)
    return dot(weights, jnp.concatenate([high, low, high], axis=0))


def split_weights(w):
    high, low = halves(w)
    return jnp.concatenate([high.astype(F32), high.astype(F32), low.astype(F32)], axis=1).astype(BF16)


def pick(source, lane):
    return jnp.take_along_axis(source, lane, axis=1, mode="promise_in_bounds")


def pick_wide(source, index):
    rows = source.shape[0]
    index = jnp.broadcast_to(index, (rows, LANES))
    lane = index & (LANES - 1)
    return jnp.where(index < LANES, pick(source[:, :LANES], lane), pick(source[:, LANES:], lane))


def gathered(traces, below, above, nbr_ref):
    rows = []
    for face in range(6):
        first = (face ^ 1) * TRACE
        source = traces[first : first + TRACE]
        parts = []
        for half in range(2):
            index = nbr_ref[face : face + 1, half * LANES : (half + 1) * LANES]
            index = jnp.broadcast_to(index, (TRACE, LANES))
            lane = index & (LANES - 1)
            value = jnp.where(index < LANES, pick(source[:, :LANES], lane), pick(source[:, LANES:], lane))
            if face < 2:
                outer = (below, above)[face]
                other = jnp.zeros((TRACE, LANES), F32) if outer is None else pick(outer, lane)
                value = jnp.where(index < 2 * LANES, value, other)
            parts.append(value)
        rows.append(jnp.concatenate(parts, axis=1))
    return jnp.concatenate(rows, axis=0)


def boundary(below, above, nbr_ref):
    rows = []
    for face, outer in enumerate((below, above)):
        parts = []
        for half in range(2):
            index = nbr_ref[face : face + 1, half * LANES : (half + 1) * LANES]
            index = jnp.broadcast_to(index, (TRACE, LANES))
            parts.append(jnp.where(index < 2 * LANES, 0.0, pick(outer, index & (LANES - 1))))
        rows.append(jnp.concatenate(parts, axis=1))
    return jnp.concatenate(rows, axis=0)


def apply_inverse(q_ref, d_ref, rows_ref, right):
    rows_ref[...] = right

    def step(chunk, total):
        for k in range(8):
            j = chunk * 8 + k
            total = total - q_ref[j] * rows_ref[pl.ds(j, 1), :]
        return total

    return lax.fori_loop(0, DOFS // 8, step, 2.0 * d_ref[...] * right)


def apply_faces(k_ref, rows_ref, right):
    rows_ref[...] = right

    def step(chunk, total):
        for k in range(8):
            u = chunk * 8 + k
            total = total + k_ref[u] * rows_ref[pl.ds(u, 1), :]
        return total

    return lax.fori_loop(0, TRACE // 8, step, jnp.zeros((TRACE, LANES), F32))


def weights_kernel(trace_ref, lift_ref, wt_ref, wl_ref, wi_ref):
    wt_ref[...] = split_weights(trace_ref[...])
    wl_ref[...] = split_weights(lift_ref[...])
    wi_ref[...] = split_weights(lift_ref[:, : 2 * TRACE])


def faces_kernel(q_ref, send_ref, tr_ref, lift_ref, d_ref, k0_ref, k1_ref, m0_ref, m1_ref):
    for i in range(DOFS):
        d_ref[i : i + 1, :] = q_ref[i, i : i + 1, :]
    tr = split_weights(tr_ref[...])
    lifts = [split_weights(lift_ref[slot]) for slot in range(2)]
    column = lax.broadcasted_iota(jnp.int32, (2 * TRACE, DOFS), 1)

    def maps(j, carry):
        here = jnp.sum(jnp.where(column == j, tr_ref[...], 0.0), axis=1, keepdims=True)
        m = 2.0 * here * d_ref[pl.ds(j, 1), :] - dot3(tr, q_ref[j])
        place = pl.ds(pl.multiple_of(j * TRACE, TRACE), TRACE)
        m0_ref[place, :] = pick_wide(m[:TRACE], send_ref[0:1, :])
        m1_ref[place, :] = pick_wide(m[TRACE:], send_ref[1:2, :])
        return carry

    lax.fori_loop(0, DOFS, maps, 0, unroll=4)

    def lift(t, carry):
        for m_ref, k_ref, w in ((m0_ref, k0_ref, lifts[0]), (m1_ref, k1_ref, lifts[1])):
            rows = m_ref[pl.ds(t, DOFS, stride=TRACE), :]
            k_ref[pl.ds(t, TRACE, stride=TRACE), :] = dot3(w, rows)
        return carry

    lax.fori_loop(0, TRACE, lift, 0, unroll=4)


def sides(scal_ref, first, second):
    even = scal_ref[0] == 0
    return jnp.where(even, second, first), jnp.where(even, first, second)


def finish(scal_ref, w, rec0_ref, rec1_ref, g_ref, b_ref, x_ref, rows_ref, face_rows_ref):
    q_ref, d_ref, k0_ref, k1_ref, nbr_ref, send_ref, wt_ref, wl_ref, wi_ref = w
    there = scal_ref[1] == 1
    rec0 = rec0_ref[...]
    rec1 = jnp.where(there, rec1_ref[...], 0.0)
    below, above = sides(scal_ref, rec0[TRACE:], rec1[TRACE:])
    outer = dot3(wi_ref[...], boundary(below, above, nbr_ref))
    v1 = apply_inverse(q_ref, d_ref, rows_ref, g_ref[...] - outer)
    traces = dot3(wt_ref[...], v1)
    next0 = rec0[:TRACE] - apply_faces(k0_ref, face_rows_ref, x_ref[:TRACE])
    next1 = rec1[:TRACE] - apply_faces(k1_ref, face_rows_ref, x_ref[TRACE:])
    below, above = sides(scal_ref, next0, jnp.where(there, next1, 0.0))
    coupled = dot3(wl_ref[...], gathered(traces, below, above, nbr_ref))
    return apply_inverse(q_ref, d_ref, rows_ref, b_ref[...] - coupled)


def begin(scal_ref, w, v, b, g_ref, x_ref, msg0_ref, msg1_ref, rows_ref):
    q_ref, d_ref, nbr_ref, send_ref, wt_ref, wl_ref = w
    even = scal_ref[0] == 0

    def leaving(traces):
        low, high = traces[:TRACE], traces[TRACE : 2 * TRACE]
        return (
            pick_wide(jnp.where(even, high, low), send_ref[0:1, :]),
            pick_wide(jnp.where(even, low, high), send_ref[1:2, :]),
        )

    traces = dot3(wt_ref[...], v)
    x0, x1 = leaving(traces)
    g = b - dot3(wl_ref[...], gathered(traces, None, None, nbr_ref))
    u = apply_inverse(q_ref, d_ref, rows_ref, g)
    w0, w1 = leaving(dot3(wt_ref[: 2 * TRACE, :], u))
    g_ref[...] = g
    x_ref[...] = jnp.concatenate([x0, x1], axis=0)
    msg0_ref[...] = jnp.concatenate([w0, x0], axis=0)
    msg1_ref[...] = jnp.concatenate([w1, x1], axis=0)


def first_kernel(scal_ref, q_ref, d_ref, nbr_ref, send_ref, wt_ref, wl_ref, anchor_ref, force_ref,
                 b_ref, g_ref, x_ref, msg0_ref, msg1_ref, rows_ref):
    v = anchor_ref[...]
    b = v + force_ref[0]
    b_ref[...] = b
    begin(scal_ref, (q_ref, d_ref, nbr_ref, send_ref, wt_ref, wl_ref), v, b, g_ref, x_ref, msg0_ref, msg1_ref, rows_ref)


def fine_kernel(step, scal_ref, q_ref, d_ref, k0_ref, k1_ref, nbr_ref, send_ref, wt_ref, wl_ref, wi_ref,
                rec0_ref, rec1_ref, bin_ref, gin_ref, xin_ref, force_ref,
                v_ref, b_ref, g_ref, x_ref, msg0_ref, msg1_ref, rows_ref, face_rows_ref):
    op = (q_ref, d_ref, k0_ref, k1_ref, nbr_ref, send_ref, wt_ref, wl_ref, wi_ref)
    v = finish(scal_ref, op, rec0_ref, rec1_ref, gin_ref, bin_ref, xin_ref, rows_ref, face_rows_ref)
    v_ref[...] = v
    b = v + force_ref[step]
    b_ref[...] = b
    begin(scal_ref, (q_ref, d_ref, nbr_ref, send_ref, wt_ref, wl_ref), v, b, g_ref, x_ref, msg0_ref, msg1_ref, rows_ref)


def last_kernel(scal_ref, q_ref, d_ref, k0_ref, k1_ref, nbr_ref, send_ref, wt_ref, wl_ref, wi_ref,
                rec0_ref, rec1_ref, bin_ref, gin_ref, xin_ref, less_ref, v_ref, rows_ref, face_rows_ref):
    op = (q_ref, d_ref, k0_ref, k1_ref, nbr_ref, send_ref, wt_ref, wl_ref, wi_ref)
    v = finish(scal_ref, op, rec0_ref, rec1_ref, gin_ref, bin_ref, xin_ref, rows_ref, face_rows_ref)
    v_ref[...] = v - less_ref[...]


def start_kernel(scal_ref, q_ref, d_ref, nbr_ref, send_ref, wt_ref, wl_ref, v_ref,
                 g_ref, x_ref, msg0_ref, msg1_ref, rows_ref):
    v = v_ref[...]
    begin(scal_ref, (q_ref, d_ref, nbr_ref, send_ref, wt_ref, wl_ref), v, v, g_ref, x_ref, msg0_ref, msg1_ref, rows_ref)


def turn_kernel(turn, more, scal_ref, q_ref, d_ref, k0_ref, k1_ref, nbr_ref, send_ref, wt_ref, wl_ref, wi_ref,
                rec0_ref, rec1_ref, bin_ref, gin_ref, xin_ref, res_ref, *refs):
    if more:
        b_ref, g_ref, x_ref, msg0_ref, msg1_ref, rows_ref, face_rows_ref = refs
    else:
        b_ref, rows_ref, face_rows_ref = refs
    op = (q_ref, d_ref, k0_ref, k1_ref, nbr_ref, send_ref, wt_ref, wl_ref, wi_ref)
    v = finish(scal_ref, op, rec0_ref, rec1_ref, gin_ref, bin_ref, xin_ref, rows_ref, face_rows_ref)
    v = v + res_ref[scal_ref[2 + turn]]
    b_ref[...] = v
    if more:
        begin(scal_ref, (q_ref, d_ref, nbr_ref, send_ref, wt_ref, wl_ref), v, v, g_ref, x_ref, msg0_ref, msg1_ref, rows_ref)


def shape(*dims, dtype=F32):
    return jax.ShapeDtypeStruct(dims, dtype)


STATE = shape(DOFS, ELEMS)
EDGE = shape(2 * TRACE, LANES)
ROWS = pltpu.VMEM((DOFS, ELEMS), F32)
FACE_ROWS = pltpu.VMEM((TRACE, LANES), F32)
BEGUN = (STATE, EDGE, EDGE, EDGE)


def call(kernel, outs, scratch, *args, scalars=True, limit=None, cost=None):
    specs = [VMEM] * len(args)
    if scalars:
        specs[0] = SMEM
    return pl.pallas_call(
        kernel,
        out_shape=outs,
        in_specs=specs,
        out_specs=[VMEM] * len(outs),
        scratch_shapes=scratch,
        compiler_params=pltpu.CompilerParams(vmem_limit_bytes=limit),
    )(*args)


def local(
    initial,
    guess,
    forcing,
    fine_inverse,
    coarse_inverse,
    neighbour,
    send_low,
    send_high,
    trace_map,
    lift_map,
):
    times = lax.axis_size("tm")
    blocks = lax.axis_size("space")
    now = lax.axis_index("tm")
    place = lax.axis_index("space")
    odd = place % 2
    guess = guess[0]

    def route(time_of, place_of):
        return [
            (t * blocks + s, time_of(t) * blocks + place_of(s))
            for t in range(times)
            for s in range(blocks)
        ]

    def other(s):
        there = s + 1 if s % 2 else s - 1
        return there if 0 <= there < blocks else s

    same = lambda i: i
    beside = [route(same, lambda s: s ^ 1), route(same, other)]

    def move(x, pairs):
        return lax.ppermute(x, ("tm", "space"), pairs)

    def exchange(first, second):
        return move(first, beside[0]), move(second, beside[1])

    def by_partner(low, high):
        return jnp.where(odd == 0, jnp.stack([high, low]), jnp.stack([low, high]))

    send = by_partner(send_low, send_high)
    tr = by_partner(trace_map[0], trace_map[1]).reshape(2 * TRACE, DOFS)
    lift_sides = by_partner(lift_map[0].T, lift_map[1].T)
    has_second = jnp.where(odd == 0, place > 0, place < blocks - 1).astype(jnp.int32)
    group, core = now % 8 // 2, now % 2
    turns = jnp.arange(8)
    slots = ((group - turns // 2) % 4) * 2 + (turns % 2 ^ core)
    scal = jnp.concatenate([jnp.stack([odd, has_second]), slots]).astype(jnp.int32)

    wt, wl, wi = call(
        weights_kernel,
        [shape(192, 192, dtype=BF16), shape(64, 576, dtype=BF16), shape(64, 192, dtype=BF16)],
        [],
        trace_map.reshape(6 * TRACE, DOFS),
        jnp.transpose(lift_map, (1, 0, 2)).reshape(DOFS, 6 * TRACE),
        scalars=False,
    )

    def operator(inverse):
        d, k0, k1 = call(
            faces_kernel,
            [STATE, shape(TRACE * TRACE, LANES), shape(TRACE * TRACE, LANES)],
            [pltpu.VMEM((DOFS * TRACE, LANES), F32)] * 2,
            inverse,
            send,
            tr,
            lift_sides,
            scalars=False,
        )
        k0, k1 = exchange(k0, k1)
        return inverse, d, k0.reshape(TRACE, TRACE, LANES), k1.reshape(TRACE, TRACE, LANES)

    ahead = [(i, i + 1) for i in range(times - 1)]
    moved = lax.ppermute(guess, "tm", ahead)
    anchor = jnp.where(now == 0, initial, moved)
    fine = operator(fine_inverse)
    coarse = operator(coarse_inverse)
    short = (neighbour, send, wt, wl)
    tables = (neighbour, send, wt, wl, wi)

    def relax(start, count, less):
        b, g, x, m0, m1 = call(
            first_kernel, [STATE, *BEGUN], [ROWS], scal, *fine[:2], *short, start, forcing
        )
        points = []
        for step in range(1, count):
            m0, m1 = exchange(m0, m1)
            v, b, g, x, m0, m1 = call(
                functools.partial(fine_kernel, step),
                [STATE, STATE, *BEGUN],
                [ROWS, FACE_ROWS],
                scal, *fine, *tables, m0, m1, b, g, x, forcing,
            )
            points.append(v)
        m0, m1 = exchange(m0, m1)
        (v,) = call(
            last_kernel, [STATE], [ROWS, FACE_ROWS], scal, *fine, *tables, m0, m1, b, g, x, less
        )
        return points + [v]

    residual = relax(anchor, 4, guess)[-1]
    partner_core = route(lambda t: t ^ 1, same)
    pair = jnp.stack([residual, move(residual, partner_core)])

    def turned(k):
        return route(lambda t: t // 8 * 8 + (t % 8 + 2 * k) % 8, same)

    held = jnp.concatenate([pair] + [move(pair, turned(k)) for k in (1, 2, 3)])

    def chain(b, first, count):
        g, x, m0, m1 = call(start_kernel, BEGUN, [ROWS], scal, *coarse[:2], *short, b)
        ends = [b]
        for turn in range(first, first + count):
            more = turn < first + count - 1
            m0, m1 = exchange(m0, m1)
            out = call(
                functools.partial(turn_kernel, turn, more),
                [STATE, *BEGUN] if more else [STATE],
                [ROWS, FACE_ROWS],
                scal, *coarse, *tables, m0, m1, b, g, x, held,
            )
            b = out[0]
            if more:
                b, g, x, m0, m1 = out
            ends.append(b)
        return ends

    early = now < 8
    turn = now % 8
    base = lax.dynamic_index_in_dim(held, scal[2], 0, False)
    early_ends = chain(base, 1, 7)
    late_ends = chain(move(early_ends[-1], route(lambda t: t ^ 8, same)), 0, 8)
    zero = jnp.zeros_like(base)
    before = jnp.where(early, jnp.where(turn == 0, zero, 0.0), late_ends[0])
    after = jnp.where(early, early_ends[0], late_ends[1])
    for k in range(1, 8):
        before = jnp.where(turn == k, jnp.where(early, early_ends[k - 1], late_ends[k]), before)
        after = jnp.where(turn == k, jnp.where(early, early_ends[k], late_ends[k + 1]), after)
    last_pass = relax(anchor + before, 3, zero)
    return jnp.stack(last_pass + [guess + after])


def solution(mesh):
    in_specs = (
        P(None, "space"),
        P("tm", None, "space"),
        P("tm", None, "space"),
        P(None, None, "space"),
        P(None, None, "space"),
        P(None, "space"),
        P("space"),
        P("space"),
        P(),
        P(),
    )
    out_specs = P("tm", None, "space")
    return jax.shard_map(local, mesh=mesh, in_specs=in_specs, out_specs=out_specs, check_vma=False)
```

time: 1170 us -> 449 us (0.38)
  local copies, waits for them, and re-layouts: 320 us -> 18.2 us
  waiting for transfers between devices: 350 us -> 94.8 us
  Pallas kernels: 0 us -> 177 us
  starting transfers between devices: 292 us -> 140 us
  other arithmetic: 159 us -> 8.86 us
  matrix products: 29.7 us -> 0 us
    gather x440 -> x0, local copies, waits for them, and re-layouts: 256 us -> none  [the longest x264 194 us: couple(): gathered.append(jnp.take(lookup, neighbour[face_index], axis=1))]
    ppermute x105 -> x54, waiting for transfers between devices: 350 us -> 94.8 us  [the longest x53 78.3 us: move(): return lax.ppermute(x, ('tm', 'space'), pairs)]
    pallas_call x0 -> x29, Pallas kernels: none -> 177 us  [call(): pl.pallas_call(kernel, out_shape=outs, in_specs=specs, out_specs=[VMEM] *...]
    ppermute x105 -> x54, starting transfers between devices: 292 us -> 140 us  [the longest x53 138 us: move(): return lax.ppermute(x, ('tm', 'space'), pairs)]
    dot_general x44 -> x0, other arithmetic: 125 us -> none  [jacobi(): jnp.einsum('ije,je->ie', inverse, right_side - coupled, precision=HIGH)]
    concatenate x264 -> x1, local copies, waits for them, and re-layouts: 34.6 us -> 0.01 us  [local(): held = jnp.concatenate([pair] + [move(pair, turned(k)) for k in (1, 2, 3)])]
    dot_general x88 -> x0, matrix products: 29.7 us -> none  [the longest x44 15.6 us: couple(): jnp.einsum('fit,fte->ie', lift_map, jnp.stack(gathered), precision=HIGH)]
    another operation x353 -> x3, other arithmetic: 27.5 us -> 3.34 us  [the longest x2 2.49 us: local(): return jnp.stack(last_pass + [guess + after])]
  transfers between devices with their start and end apart: 105 -> 54, of which waited for: 61 -> 23; matrix products, arithmetic and copies ran while one was open for 4% -> 1% of each run, Pallas kernels for 0% -> 9%
where the time goes in v1:
time: 449 us; the launch traced here: 441 us
  Pallas kernels  177 us (39%)
  starting transfers between devices  140 us (31%)
  waiting for transfers between devices  94.8 us (21%)
  local copies, waits for them, and re-layouts  18.2 us (4%)
  other arithmetic  8.86 us (2%)
    pallas_call x29, Pallas kernels, call(): pl.pallas_call(kernel, out_shape=outs, in_specs=specs, out_specs=[VMEM] *...  177 us
    ppermute x53, starting transfers between devices, move(): return lax.ppermute(x, ('tm', 'space'), pairs)  138 us
    ppermute x53, waiting for transfers between devices, move(): return lax.ppermute(x, ('tm', 'space'), pairs)  78.3 us
    ppermute x1, waiting for transfers between devices, local(): moved = lax.ppermute(guess, 'tm', ahead)  16.5 us
    unnamed x154, local copies, waits for them, and re-layouts  14.6 us
  transfers between devices with their start and end apart: 54, of which 23 were waited for; matrix products, arithmetic and copies ran while one was open for 1% of the time, Pallas kernels for 9%

profile of v1, /device:TPU:134, one launch (start us, length us, event | category | flops | bytes accessed | tf_op | source)
XLA Modules:
  0.0 440.6 jit_solution(10003770398851972355)
XLA Ops:
  4.3 13.1 %shard_map.100 = (f32[64,256]{1,0:T(8,128)}, f32[1024,128]{1,0:T(8,128)}, f32[1024,128]{1,0:T(8,128)}) custom-call(f32[64,64,256]{2,1,0:T(8,128)} %q_ref.54, s32[2,128]{1,0:T(2,128)} %add_select_fusion.send_ref, f32[64,64]{1,0:T(8,128)} %bitcast.89, f32[2,32,64]{2,1,0:T(8,128)} %get-tuple-element.248.lift_ref), custom_call_target="tpu_custom_call" | custom-call | tf_op jit(solution)/shard_map/pallas_call | solution.py:243
  27.4 16.5 %collective-permute-done.2 = f32[64,256]{1,0:T(8,128)S(1)} collective-permute-done((f32[64,256]{1,0:T(8,128)S(1)}, f32[64,256]{1,0:T(8,128)S(1)}, u32[]{:S(2)}, u32[]{:S(2)}) %collective-permute-start.2) | collective-permute-done | bytes 65568 | tf_op jit(solution)/shard_map/ppermute | solution.py:328
  48.7 7.9 %collective-permute-start.6 = (f32[64,128]{1,0:T(8,128)}, f32[64,128]{1,0:T(8,128)S(1)}, u32[]{:S(2)}, u32[]{:S(2)}) collective-permute-start(f32[64,128]{1,0:T(8,128)} %get-tuple-element.134), channel_id=1, source_target_pairs={{0,0},{1,2},{2,1},{3,4},{4,3},{5,6},{6,5},{7,8},{8,7},{9,10},{10,9... | collective-permute-start | bytes 98312 | tf_op jit(solution)/shard_map/ppermute | solution.py:287
  59.7 6.2 %shard_map.104 = (f32[64,256]{1,0:T(8,128)}, f32[64,256]{1,0:T(8,128)}, f32[64,256]{1,0:T(8,128)}, f32[64,128]{1,0:T(8,128)}, f32[64,128]{1,0:T(8,128)}, /*index=5*/f32[64,128]{1,0:T(8,128)}) custom-call(s32[10]{0:T(128)} %pad_add_fusion.scal_ref, f32[64,64,256]{2,1,0:T(8,128)} %q_ref.54, f32[64,256]{1,0:T(8,128)} %get-tuple-element.124.d_ref, ...), custom_call_target="tpu_custom_call" | custom-call | tf_op jit(solution)/shard_map/pallas_call | solution.py:243
  65.9 6.6 %collective-permute-start.8 = (f32[64,128]{1,0:T(8,128)}, f32[64,128]{1,0:T(8,128)S(1)}, u32[]{:S(2)}, u32[]{:S(2)}) collective-permute-start(f32[64,128]{1,0:T(8,128)} %get-tuple-element.139), channel_id=1, source_target_pairs={{0,0},{1,2},{2,1},{3,4},{4,3},{5,6},{6,5},{7,8},{8,7},{9,10},{10,9... | collective-permute-start | bytes 98312 | tf_op jit(solution)/shard_map/ppermute | solution.py:287
  75.3 6.2 %shard_map.105 = (f32[64,256]{1,0:T(8,128)}, f32[64,256]{1,0:T(8,128)}, f32[64,256]{1,0:T(8,128)}, f32[64,128]{1,0:T(8,128)}, f32[64,128]{1,0:T(8,128)}, /*index=5*/f32[64,128]{1,0:T(8,128)}) custom-call(s32[10]{0:T(128)} %pad_add_fusion.scal_ref, f32[64,64,256]{2,1,0:T(8,128)} %q_ref.54, f32[64,256]{1,0:T(8,128)} %get-tuple-element.124.d_ref, ...), custom_call_target="tpu_custom_call" | custom-call | tf_op jit(solution)/shard_map/pallas_call | solution.py:243
  81.5 6.6 %collective-permute-start.10 = (f32[64,128]{1,0:T(8,128)}, f32[64,128]{1,0:T(8,128)S(1)}, u32[]{:S(2)}, u32[]{:S(2)}) collective-permute-start(f32[64,128]{1,0:T(8,128)} %get-tuple-element.144), channel_id=1, source_target_pairs={{0,0},{1,2},{2,1},{3,4},{4,3},{5,6},{6,5},{7,8},{8,7},{9,10},{10,9... | collective-permute-start | bytes 98312 | tf_op jit(solution)/shard_map/ppermute | solution.py:287
  90.8 6.2 %shard_map.106 = (f32[64,256]{1,0:T(8,128)}, f32[64,256]{1,0:T(8,128)}, f32[64,256]{1,0:T(8,128)}, f32[64,128]{1,0:T(8,128)}, f32[64,128]{1,0:T(8,128)}, /*index=5*/f32[64,128]{1,0:T(8,128)}) custom-call(s32[10]{0:T(128)} %pad_add_fusion.scal_ref, f32[64,64,256]{2,1,0:T(8,128)} %q_ref.54, f32[64,256]{1,0:T(8,128)} %get-tuple-element.124.d_ref, ...), custom_call_target="tpu_custom_call" | custom-call | tf_op jit(solution)/shard_map/pallas_call | solution.py:243
  97.1 6.6 %collective-permute-start.12 = (f32[64,128]{1,0:T(8,128)}, f32[64,128]{1,0:T(8,128)S(1)}, u32[]{:S(2)}, u32[]{:S(2)}) collective-permute-start(f32[64,128]{1,0:T(8,128)} %get-tuple-element.149), channel_id=1, source_target_pairs={{0,0},{1,2},{2,1},{3,4},{4,3},{5,6},{6,5},{7,8},{8,7},{9,10},{10,9... | collective-permute-start | bytes 98312 | tf_op jit(solution)/shard_map/ppermute | solution.py:287
  103.7 13.1 %shard_map.102 = (f32[64,256]{1,0:T(8,128)}, f32[1024,128]{1,0:T(8,128)}, f32[1024,128]{1,0:T(8,128)}) custom-call(f32[64,64,256]{2,1,0:T(8,128)} %q_ref.55, s32[2,128]{1,0:T(2,128)} %add_select_fusion.send_ref, f32[64,64]{1,0:T(8,128)} %bitcast.90, f32[2,32,64]{2,1,0:T(8,128)} %get-tuple-element.248.lift_ref), custom_call_target="tpu_custom_call" | custom-call | tf_op jit(solution)/shard_map/pallas_call | solution.py:243
  132.2 6.1 %collective-permute-done.14 = f32[2,64,256]{2,1,0:T(8,128)S(1)} collective-permute-done((f32[2,64,256]{2,1,0:T(8,128)S(1)}, f32[2,64,256]{2,1,0:T(8,128)S(1)}, u32[]{:S(2)}, u32[]{:S(2)}) %collective-permute-start.14) | collective-permute-done | bytes 131104 | tf_op jit(solution)/shard_map/ppermute | solution.py:287
  153.1 6.3 %shard_map.109 = (f32[64,256]{1,0:T(8,128)}, f32[64,256]{1,0:T(8,128)}, f32[64,128]{1,0:T(8,128)}, f32[64,128]{1,0:T(8,128)}, f32[64,128]{1,0:T(8,128)}) custom-call(s32[10]{0:T(128)} %pad_add_fusion.scal_ref, f32[64,64,256]{2,1,0:T(8,128)} %q_ref.55, f32[64,256]{1,0:T(8,128)} %get-tuple-element.130.d_ref, f32[32,32,128]{2,1,0:T(8,128)} %bitcast.44, ...), custom_call_target="tpu_custom_call" | custom-call | tf_op jit(solution)/shard_map/pallas_call | solution.py:243
  168.7 6.3 %shard_map.110 = (f32[64,256]{1,0:T(8,128)}, f32[64,256]{1,0:T(8,128)}, f32[64,128]{1,0:T(8,128)}, f32[64,128]{1,0:T(8,128)}, f32[64,128]{1,0:T(8,128)}) custom-call(s32[10]{0:T(128)} %pad_add_fusion.scal_ref, f32[64,64,256]{2,1,0:T(8,128)} %q_ref.55, f32[64,256]{1,0:T(8,128)} %get-tuple-element.130.d_ref, f32[32,32,128]{2,1,0:T(8,128)} %bitcast.45, ...), custom_call_target="tpu_custom_call" | custom-call | tf_op jit(solution)/shard_map/pallas_call | solution.py:243
  184.3 6.3 %shard_map.111 = (f32[64,256]{1,0:T(8,128)}, f32[64,256]{1,0:T(8,128)}, f32[64,128]{1,0:T(8,128)}, f32[64,128]{1,0:T(8,128)}, f32[64,128]{1,0:T(8,128)}) custom-call(s32[10]{0:T(128)} %pad_add_fusion.scal_ref, f32[64,64,256]{2,1,0:T(8,128)} %q_ref.55, f32[64,256]{1,0:T(8,128)} %get-tuple-element.130.d_ref, f32[32,32,128]{2,1,0:T(8,128)} %bitcast.46, ...), custom_call_target="tpu_custom_call" | custom-call | tf_op jit(solution)/shard_map/pallas_call | solution.py:243
  200.0 6.3 %shard_map.112 = (f32[64,256]{1,0:T(8,128)}, f32[64,256]{1,0:T(8,128)}, f32[64,128]{1,0:T(8,128)}, f32[64,128]{1,0:T(8,128)}, f32[64,128]{1,0:T(8,128)}) custom-call(s32[10]{0:T(128)} %pad_add_fusion.scal_ref, f32[64,64,256]{2,1,0:T(8,128)} %q_ref.55, f32[64,256]{1,0:T(8,128)} %get-tuple-element.130.d_ref, f32[32,32,128]{2,1,0:T(8,128)} %bitcast.47, ...), custom_call_target="tpu_custom_call" | custom-call | tf_op jit(solution)/shard_map/pallas_call | solution.py:243
  215.6 6.3 %shard_map.113 = (f32[64,256]{1,0:T(8,128)}, f32[64,256]{1,0:T(8,128)}, f32[64,128]{1,0:T(8,128)}, f32[64,128]{1,0:T(8,128)}, f32[64,128]{1,0:T(8,128)}) custom-call(s32[10]{0:T(128)} %pad_add_fusion.scal_ref, f32[64,64,256]{2,1,0:T(8,128)} %q_ref.55, f32[64,256]{1,0:T(8,128)} %get-tuple-element.130.d_ref, f32[32,32,128]{2,1,0:T(8,128)} %bitcast.48, ...), custom_call_target="tpu_custom_call" | custom-call | tf_op jit(solution)/shard_map/pallas_call | solution.py:243
  231.2 6.3 %shard_map.114 = (f32[64,256]{1,0:T(8,128)}, f32[64,256]{1,0:T(8,128)}, f32[64,128]{1,0:T(8,128)}, f32[64,128]{1,0:T(8,128)}, f32[64,128]{1,0:T(8,128)}) custom-call(s32[10]{0:T(128)} %pad_add_fusion.scal_ref, f32[64,64,256]{2,1,0:T(8,128)} %q_ref.55, f32[64,256]{1,0:T(8,128)} %get-tuple-element.130.d_ref, f32[32,32,128]{2,1,0:T(8,128)} %bitcast.49, ...), custom_call_target="tpu_custom_call" | custom-call | tf_op jit(solution)/shard_map/pallas_call | solution.py:243
  246.8 5.1 %shard_map.115 = f32[64,256]{1,0:T(8,128)} custom-call(s32[10]{0:T(128)} %pad_add_fusion.scal_ref, f32[64,64,256]{2,1,0:T(8,128)} %q_ref.55, f32[64,256]{1,0:T(8,128)} %get-tuple-element.130.d_ref, f32[32,32,128]{2,1,0:T(8,128)} %bitcast.50, f32[32,32,128]{2,1,0:T(8,128)} %bitcast.65, s32[6,256]{1,0:T(8,128)} %nbr_ref.51, s32[2,128]{1,0:T(2,128)} %add_select_fusion.send_ref, ...), custom_call_target="tpu_custom_call" | custom-call | tf_op jit(solution)/shard_map/pallas_call | solution.py:243
  251.9 8.4 %collective-permute-done.31.v_ref.bin_ref = f32[64,256]{1,0:T(8,128)S(1)} collective-permute-done((f32[64,256]{1,0:T(8,128)}, f32[64,256]{1,0:T(8,128)S(1)}, u32[]{:S(2)}, u32[]{:S(2)}) %collective-permute-start.31) | collective-permute-done | bytes 65568 | tf_op jit(solution)/shard_map/ppermute | solution.py:287
  265.0 8.6 %collective-permute-start.32 = (f32[64,128]{1,0:T(8,128)}, f32[64,128]{1,0:T(8,128)S(1)}, u32[]{:S(2)}, u32[]{:S(2)}) collective-permute-start(f32[64,128]{1,0:T(8,128)} %get-tuple-element.187), channel_id=1, source_target_pairs={{0,1},{1,0},{2,3},{3,2},{4,5},{5,4},{6,7},{7,6},{8,9},{9,8},{10,11... | collective-permute-start | bytes 98312 | tf_op jit(solution)/shard_map/ppermute | solution.py:287
  273.6 5.2 %collective-permute-start.33 = (f32[64,128]{1,0:T(8,128)}, f32[64,128]{1,0:T(8,128)S(1)}, u32[]{:S(2)}, u32[]{:S(2)}) collective-permute-start(f32[64,128]{1,0:T(8,128)} %get-tuple-element.188), channel_id=1, source_target_pairs={{0,0},{1,2},{2,1},{3,4},{4,3},{5,6},{6,5},{7,8},{8,7},{9,10},{10,9... | collective-permute-start | bytes 98312 | tf_op jit(solution)/shard_map/ppermute | solution.py:287
  283.1 6.3 %shard_map.117 = (f32[64,256]{1,0:T(8,128)}, f32[64,256]{1,0:T(8,128)}, f32[64,128]{1,0:T(8,128)}, f32[64,128]{1,0:T(8,128)}, f32[64,128]{1,0:T(8,128)}) custom-call(s32[10]{0:T(128)} %pad_add_fusion.scal_ref, f32[64,64,256]{2,1,0:T(8,128)} %q_ref.55, f32[64,256]{1,0:T(8,128)} %get-tuple-element.130.d_ref, f32[32,32,128]{2,1,0:T(8,128)} %bitcast.51, ...), custom_call_target="tpu_custom_call" | custom-call | tf_op jit(solution)/shard_map/pallas_call | solution.py:243
  298.7 6.3 %shard_map.118 = (f32[64,256]{1,0:T(8,128)}, f32[64,256]{1,0:T(8,128)}, f32[64,128]{1,0:T(8,128)}, f32[64,128]{1,0:T(8,128)}, f32[64,128]{1,0:T(8,128)}) custom-call(s32[10]{0:T(128)} %pad_add_fusion.scal_ref, f32[64,64,256]{2,1,0:T(8,128)} %q_ref.55, f32[64,256]{1,0:T(8,128)} %get-tuple-element.130.d_ref, f32[32,32,128]{2,1,0:T(8,128)} %bitcast.52, ...), custom_call_target="tpu_custom_call" | custom-call | tf_op jit(solution)/shard_map/pallas_call | solution.py:243
  314.4 6.3 %shard_map.119 = (f32[64,256]{1,0:T(8,128)}, f32[64,256]{1,0:T(8,128)}, f32[64,128]{1,0:T(8,128)}, f32[64,128]{1,0:T(8,128)}, f32[64,128]{1,0:T(8,128)}) custom-call(s32[10]{0:T(128)} %pad_add_fusion.scal_ref, f32[64,64,256]{2,1,0:T(8,128)} %q_ref.55, f32[64,256]{1,0:T(8,128)} %get-tuple-element.130.d_ref, f32[32,32,128]{2,1,0:T(8,128)} %bitcast.53, ...), custom_call_target="tpu_custom_call" | custom-call | tf_op jit(solution)/shard_map/pallas_call | solution.py:243
  330.0 6.3 %shard_map.120 = (f32[64,256]{1,0:T(8,128)}, f32[64,256]{1,0:T(8,128)}, f32[64,128]{1,0:T(8,128)}, f32[64,128]{1,0:T(8,128)}, f32[64,128]{1,0:T(8,128)}) custom-call(s32[10]{0:T(128)} %pad_add_fusion.scal_ref, f32[64,64,256]{2,1,0:T(8,128)} %q_ref.55, f32[64,256]{1,0:T(8,128)} %get-tuple-element.130.d_ref, f32[32,32,128]{2,1,0:T(8,128)} %bitcast.54, ...), custom_call_target="tpu_custom_call" | custom-call | tf_op jit(solution)/shard_map/pallas_call | solution.py:243
  345.7 6.3 %shard_map.121 = (f32[64,256]{1,0:T(8,128)}, f32[64,256]{1,0:T(8,128)}, f32[64,128]{1,0:T(8,128)}, f32[64,128]{1,0:T(8,128)}, f32[64,128]{1,0:T(8,128)}) custom-call(s32[10]{0:T(128)} %pad_add_fusion.scal_ref, f32[64,64,256]{2,1,0:T(8,128)} %q_ref.55, f32[64,256]{1,0:T(8,128)} %get-tuple-element.130.d_ref, f32[32,32,128]{2,1,0:T(8,128)} %bitcast.55, ...), custom_call_target="tpu_custom_call" | custom-call | tf_op jit(solution)/shard_map/pallas_call | solution.py:243
  361.3 6.3 %shard_map.122 = (f32[64,256]{1,0:T(8,128)}, f32[64,256]{1,0:T(8,128)}, f32[64,128]{1,0:T(8,128)}, f32[64,128]{1,0:T(8,128)}, f32[64,128]{1,0:T(8,128)}) custom-call(s32[10]{0:T(128)} %pad_add_fusion.scal_ref, f32[64,64,256]{2,1,0:T(8,128)} %q_ref.55, f32[64,256]{1,0:T(8,128)} %get-tuple-element.130.d_ref, f32[32,32,128]{2,1,0:T(8,128)} %bitcast.56, ...), custom_call_target="tpu_custom_call" | custom-call | tf_op jit(solution)/shard_map/pallas_call | solution.py:243
  367.8 5.1 %collective-permute-start.45 = (f32[64,128]{1,0:T(8,128)}, f32[64,128]{1,0:T(8,128)S(1)}, u32[]{:S(2)}, u32[]{:S(2)}) collective-permute-start(f32[64,128]{1,0:T(8,128)} %get-tuple-element.217), channel_id=1, source_target_pairs={{0,0},{1,2},{2,1},{3,4},{4,3},{5,6},{6,5},{7,8},{8,7},{9,10},{10,9... | collective-permute-start | bytes 98312 | tf_op jit(solution)/shard_map/ppermute | solution.py:287
  377.3 6.3 %shard_map.123 = (f32[64,256]{1,0:T(8,128)}, f32[64,256]{1,0:T(8,128)}, f32[64,128]{1,0:T(8,128)}, f32[64,128]{1,0:T(8,128)}, f32[64,128]{1,0:T(8,128)}) custom-call(s32[10]{0:T(128)} %pad_add_fusion.scal_ref, f32[64,64,256]{2,1,0:T(8,128)} %q_ref.55, f32[64,256]{1,0:T(8,128)} %get-tuple-element.130.d_ref, f32[32,32,128]{2,1,0:T(8,128)} %bitcast.57, ...), custom_call_target="tpu_custom_call" | custom-call | tf_op jit(solution)/shard_map/pallas_call | solution.py:243
  399.5 6.2 %shard_map.125 = (f32[64,256]{1,0:T(8,128)}, f32[64,256]{1,0:T(8,128)}, f32[64,256]{1,0:T(8,128)}, f32[64,128]{1,0:T(8,128)}, f32[64,128]{1,0:T(8,128)}, /*index=5*/f32[64,128]{1,0:T(8,128)}) custom-call(s32[10]{0:T(128)} %pad_add_fusion.scal_ref, f32[64,64,256]{2,1,0:T(8,128)} %q_ref.54, f32[64,256]{1,0:T(8,128)} %get-tuple-element.124.d_ref, ...), custom_call_target="tpu_custom_call" | custom-call | tf_op jit(solution)/shard_map/pallas_call | solution.py:243
  405.7 6.1 %collective-permute-start.49 = (f32[64,128]{1,0:T(8,128)}, f32[64,128]{1,0:T(8,128)S(1)}, u32[]{:S(2)}, u32[]{:S(2)}) collective-permute-start(f32[64,128]{1,0:T(8,128)} %get-tuple-element.229), channel_id=1, source_target_pairs={{0,0},{1,2},{2,1},{3,4},{4,3},{5,6},{6,5},{7,8},{8,7},{9,10},{10,9... | collective-permute-start | bytes 98312 | tf_op jit(solution)/shard_map/ppermute | solution.py:287
  418.2 6.2 %shard_map.126 = (f32[64,256]{1,0:T(8,128)}, f32[64,256]{1,0:T(8,128)}, f32[64,256]{1,0:T(8,128)}, f32[64,128]{1,0:T(8,128)}, f32[64,128]{1,0:T(8,128)}, /*index=5*/f32[64,128]{1,0:T(8,128)}) custom-call(s32[10]{0:T(128)} %pad_add_fusion.scal_ref, f32[64,64,256]{2,1,0:T(8,128)} %q_ref.54, f32[64,256]{1,0:T(8,128)} %get-tuple-element.124.d_ref, ...), custom_call_target="tpu_custom_call" | custom-call | tf_op jit(solution)/shard_map/pallas_call | solution.py:243
  (274 shorter events, 211.0 us)
Async XLA Ops:
  17.3 41.4 %collective-permute-start = (f32[1024,128]{1,0:T(8,128)}, f32[1024,128]{1,0:T(8,128)S(1)}, u32[]{:S(2)}, u32[]{:S(2)}) collective-permute-start(f32[1024,128]{1,0:T(8,128)} %get-tuple-element.125), channel_id=1, source_target_pairs={{0,1},{1,0},{2,3},{3,2},{4,5},{5,4},{6,7},{7,6},{8,9},{9,8},{10,11... | collective-permute-start | bytes 1572872 | tf_op jit(solution)/shard_map/ppermute | solution.py:287
  18.4 40.3 %collective-permute-start.1 = (f32[1024,128]{1,0:T(8,128)}, f32[1024,128]{1,0:T(8,128)S(1)}, u32[]{:S(2)}, u32[]{:S(2)}) collective-permute-start(f32[1024,128]{1,0:T(8,128)} %get-tuple-element.126), channel_id=1, source_target_pairs={{0,0},{1,2},{2,1},{3,4},{4,3},{5,6},{6,5},{7,8},{8,7},{9,10},{10,9... | collective-permute-start | bytes 1572872 | tf_op jit(solution)/shard_map/ppermute | solution.py:287
  22.5 21.4 %collective-permute-start.2 = (f32[64,256]{1,0:T(8,128)S(1)}, f32[64,256]{1,0:T(8,128)S(1)}, u32[]{:S(2)}, u32[]{:S(2)}) collective-permute-start(f32[64,256]{1,0:T(8,128)S(1)} %bitcast.93), channel_id=1, source_target_pairs={{0,16},{16,32},{32,48},{48,64},{64,80},{80,96},{96,112},{112,128},... | collective-permute-start | bytes 196616 | tf_op jit(solution)/shard_map/ppermute | solution.py:328
  48.7 10.0 %collective-permute-start.6 = (f32[64,128]{1,0:T(8,128)}, f32[64,128]{1,0:T(8,128)S(1)}, u32[]{:S(2)}, u32[]{:S(2)}) collective-permute-start(f32[64,128]{1,0:T(8,128)} %get-tuple-element.134), channel_id=1, source_target_pairs={{0,0},{1,2},{2,1},{3,4},{4,3},{5,6},{6,5},{7,8},{8,7},{9,10},{10,9... | collective-permute-start | bytes 98312 | tf_op jit(solution)/shard_map/ppermute | solution.py:287
  65.9 8.7 %collective-permute-start.8 = (f32[64,128]{1,0:T(8,128)}, f32[64,128]{1,0:T(8,128)S(1)}, u32[]{:S(2)}, u32[]{:S(2)}) collective-permute-start(f32[64,128]{1,0:T(8,128)} %get-tuple-element.139), channel_id=1, source_target_pairs={{0,0},{1,2},{2,1},{3,4},{4,3},{5,6},{6,5},{7,8},{8,7},{9,10},{10,9... | collective-permute-start | bytes 98312 | tf_op jit(solution)/shard_map/ppermute | solution.py:287
  81.5 8.7 %collective-permute-start.10 = (f32[64,128]{1,0:T(8,128)}, f32[64,128]{1,0:T(8,128)S(1)}, u32[]{:S(2)}, u32[]{:S(2)}) collective-permute-start(f32[64,128]{1,0:T(8,128)} %get-tuple-element.144), channel_id=1, source_target_pairs={{0,0},{1,2},{2,1},{3,4},{4,3},{5,6},{6,5},{7,8},{8,7},{9,10},{10,9... | collective-permute-start | bytes 98312 | tf_op jit(solution)/shard_map/ppermute | solution.py:287
  97.1 23.7 %collective-permute-start.11 = (f32[64,128]{1,0:T(8,128)}, f32[64,128]{1,0:T(8,128)S(1)}, u32[]{:S(2)}, u32[]{:S(2)}) collective-permute-start(f32[64,128]{1,0:T(8,128)} %get-tuple-element.148), channel_id=1, source_target_pairs={{0,1},{1,0},{2,3},{3,2},{4,5},{5,4},{6,7},{7,6},{8,9},{9,8},{10,11... | collective-permute-start | bytes 98312 | tf_op jit(solution)/shard_map/ppermute | solution.py:287
  97.1 23.7 %collective-permute-start.12 = (f32[64,128]{1,0:T(8,128)}, f32[64,128]{1,0:T(8,128)S(1)}, u32[]{:S(2)}, u32[]{:S(2)}) collective-permute-start(f32[64,128]{1,0:T(8,128)} %get-tuple-element.149), channel_id=1, source_target_pairs={{0,0},{1,2},{2,1},{3,4},{4,3},{5,6},{6,5},{7,8},{8,7},{9,10},{10,9... | collective-permute-start | bytes 98312 | tf_op jit(solution)/shard_map/ppermute | solution.py:287
  116.8 31.8 %collective-permute-start.3 = (f32[1024,128]{1,0:T(8,128)}, f32[1024,128]{1,0:T(8,128)S(1)}, u32[]{:S(2)}, u32[]{:S(2)}) collective-permute-start(f32[1024,128]{1,0:T(8,128)} %get-tuple-element.131), channel_id=1, source_target_pairs={{0,1},{1,0},{2,3},{3,2},{4,5},{5,4},{6,7},{7,6},{8,9},{9,8},{10,11... | collective-permute-start | bytes 1572872 | tf_op jit(solution)/shard_map/ppermute | solution.py:287
  116.8 31.8 %collective-permute-start.4 = (f32[1024,128]{1,0:T(8,128)}, f32[1024,128]{1,0:T(8,128)S(1)}, u32[]{:S(2)}, u32[]{:S(2)}) collective-permute-start(f32[1024,128]{1,0:T(8,128)} %get-tuple-element.132), channel_id=1, source_target_pairs={{0,0},{1,2},{2,1},{3,4},{4,3},{5,6},{6,5},{7,8},{8,7},{9,10},{10,9... | collective-permute-start | bytes 1572872 | tf_op jit(solution)/shard_map/ppermute | solution.py:287
  128.7 9.7 %collective-permute-start.14 = (f32[2,64,256]{2,1,0:T(8,128)S(1)}, f32[2,64,256]{2,1,0:T(8,128)S(1)}, u32[]{:S(2)}, u32[]{:S(2)}) collective-permute-start(f32[2,64,256]{2,1,0:T(8,128)S(1)} %pad_maximum_fusion.1), channel_id=1, source_target_pairs={{0,32},{1,33},{2,34},{3,35},{4,36},{5,37},{6,38},{7,39},{8,40},{9,... | collective-permute-start | bytes 393224 | tf_op jit(solution)/shard_map/ppermute | solution.py:287
  128.8 9.6 %collective-permute-start.15 = (f32[2,64,256]{2,1,0:T(8,128)S(1)}, f32[2,64,256]{2,1,0:T(8,128)S(1)}, u32[]{:S(2)}, u32[]{:S(2)}) collective-permute-start(f32[2,64,256]{2,1,0:T(8,128)S(1)} %pad_maximum_fusion.1), channel_id=1, source_target_pairs={{0,64},{1,65},{2,66},{3,67},{4,68},{5,69},{6,70},{7,71},{8,72},{9,... | collective-permute-start | bytes 393224 | tf_op jit(solution)/shard_map/ppermute | solution.py:287
  128.9 10.1 %collective-permute-start.16 = (f32[2,64,256]{2,1,0:T(8,128)S(1)}, f32[2,64,256]{2,1,0:T(8,128)S(1)}, u32[]{:S(2)}, u32[]{:S(2)}) collective-permute-start(f32[2,64,256]{2,1,0:T(8,128)S(1)} %pad_maximum_fusion.1), channel_id=1, source_target_pairs={{0,96},{1,97},{2,98},{3,99},{4,100},{5,101},{6,102},{7,103},{8,104... | collective-permute-start | bytes 393224 | tf_op jit(solution)/shard_map/ppermute | solution.py:287
  159.4 8.7 %collective-permute-start.20 = (f32[64,128]{1,0:T(8,128)}, f32[64,128]{1,0:T(8,128)S(1)}, u32[]{:S(2)}, u32[]{:S(2)}) collective-permute-start(f32[64,128]{1,0:T(8,128)} %get-tuple-element.158), channel_id=1, source_target_pairs={{0,0},{1,2},{2,1},{3,4},{4,3},{5,6},{6,5},{7,8},{8,7},{9,10},{10,9... | collective-permute-start | bytes 98312 | tf_op jit(solution)/shard_map/ppermute | solution.py:287
  175.0 8.7 %collective-permute-start.22 = (f32[64,128]{1,0:T(8,128)}, f32[64,128]{1,0:T(8,128)S(1)}, u32[]{:S(2)}, u32[]{:S(2)}) collective-permute-start(f32[64,128]{1,0:T(8,128)} %get-tuple-element.163), channel_id=1, source_target_pairs={{0,0},{1,2},{2,1},{3,4},{4,3},{5,6},{6,5},{7,8},{8,7},{9,10},{10,9... | collective-permute-start | bytes 98312 | tf_op jit(solution)/shard_map/ppermute | solution.py:287
  190.6 8.7 %collective-permute-start.24 = (f32[64,128]{1,0:T(8,128)}, f32[64,128]{1,0:T(8,128)S(1)}, u32[]{:S(2)}, u32[]{:S(2)}) collective-permute-start(f32[64,128]{1,0:T(8,128)} %get-tuple-element.168), channel_id=1, source_target_pairs={{0,0},{1,2},{2,1},{3,4},{4,3},{5,6},{6,5},{7,8},{8,7},{9,10},{10,9... | collective-permute-start | bytes 98312 | tf_op jit(solution)/shard_map/ppermute | solution.py:287
  206.3 8.7 %collective-permute-start.26 = (f32[64,128]{1,0:T(8,128)}, f32[64,128]{1,0:T(8,128)S(1)}, u32[]{:S(2)}, u32[]{:S(2)}) collective-permute-start(f32[64,128]{1,0:T(8,128)} %get-tuple-element.173), channel_id=1, source_target_pairs={{0,0},{1,2},{2,1},{3,4},{4,3},{5,6},{6,5},{7,8},{8,7},{9,10},{10,9... | collective-permute-start | bytes 98312 | tf_op jit(solution)/shard_map/ppermute | solution.py:287
  221.9 8.7 %collective-permute-start.28 = (f32[64,128]{1,0:T(8,128)}, f32[64,128]{1,0:T(8,128)S(1)}, u32[]{:S(2)}, u32[]{:S(2)}) collective-permute-start(f32[64,128]{1,0:T(8,128)} %get-tuple-element.178), channel_id=1, source_target_pairs={{0,0},{1,2},{2,1},{3,4},{4,3},{5,6},{6,5},{7,8},{8,7},{9,10},{10,9... | collective-permute-start | bytes 98312 | tf_op jit(solution)/shard_map/ppermute | solution.py:287
  237.5 8.7 %collective-permute-start.30 = (f32[64,128]{1,0:T(8,128)}, f32[64,128]{1,0:T(8,128)S(1)}, u32[]{:S(2)}, u32[]{:S(2)}) collective-permute-start(f32[64,128]{1,0:T(8,128)} %get-tuple-element.184), channel_id=1, source_target_pairs={{0,0},{1,2},{2,1},{3,4},{4,3},{5,6},{6,5},{7,8},{8,7},{9,10},{10,9... | collective-permute-start | bytes 98312 | tf_op jit(solution)/shard_map/ppermute | solution.py:287
  265.0 13.8 %collective-permute-start.32 = (f32[64,128]{1,0:T(8,128)}, f32[64,128]{1,0:T(8,128)S(1)}, u32[]{:S(2)}, u32[]{:S(2)}) collective-permute-start(f32[64,128]{1,0:T(8,128)} %get-tuple-element.187), channel_id=1, source_target_pairs={{0,1},{1,0},{2,3},{3,2},{4,5},{5,4},{6,7},{7,6},{8,9},{9,8},{10,11... | collective-permute-start | bytes 98312 | tf_op jit(solution)/shard_map/ppermute | solution.py:287
  273.6 8.9 %collective-permute-start.33 = (f32[64,128]{1,0:T(8,128)}, f32[64,128]{1,0:T(8,128)S(1)}, u32[]{:S(2)}, u32[]{:S(2)}) collective-permute-start(f32[64,128]{1,0:T(8,128)} %get-tuple-element.188), channel_id=1, source_target_pairs={{0,0},{1,2},{2,1},{3,4},{4,3},{5,6},{6,5},{7,8},{8,7},{9,10},{10,9... | collective-permute-start | bytes 98312 | tf_op jit(solution)/shard_map/ppermute | solution.py:287
  289.4 8.7 %collective-permute-start.35 = (f32[64,128]{1,0:T(8,128)}, f32[64,128]{1,0:T(8,128)S(1)}, u32[]{:S(2)}, u32[]{:S(2)}) collective-permute-start(f32[64,128]{1,0:T(8,128)} %get-tuple-element.192), channel_id=1, source_target_pairs={{0,0},{1,2},{2,1},{3,4},{4,3},{5,6},{6,5},{7,8},{8,7},{9,10},{10,9... | collective-permute-start | bytes 98312 | tf_op jit(solution)/shard_map/ppermute | solution.py:287
  305.0 8.7 %collective-permute-start.37 = (f32[64,128]{1,0:T(8,128)}, f32[64,128]{1,0:T(8,128)S(1)}, u32[]{:S(2)}, u32[]{:S(2)}) collective-permute-start(f32[64,128]{1,0:T(8,128)} %get-tuple-element.197), channel_id=1, source_target_pairs={{0,0},{1,2},{2,1},{3,4},{4,3},{5,6},{6,5},{7,8},{8,7},{9,10},{10,9... | collective-permute-start | bytes 98312 | tf_op jit(solution)/shard_map/ppermute | solution.py:287
  320.7 8.8 %collective-permute-start.39 = (f32[64,128]{1,0:T(8,128)}, f32[64,128]{1,0:T(8,128)S(1)}, u32[]{:S(2)}, u32[]{:S(2)}) collective-permute-start(f32[64,128]{1,0:T(8,128)} %get-tuple-element.202), channel_id=1, source_target_pairs={{0,0},{1,2},{2,1},{3,4},{4,3},{5,6},{6,5},{7,8},{8,7},{9,10},{10,9... | collective-permute-start | bytes 98312 | tf_op jit(solution)/shard_map/ppermute | solution.py:287
  336.4 8.7 %collective-permute-start.41 = (f32[64,128]{1,0:T(8,128)}, f32[64,128]{1,0:T(8,128)S(1)}, u32[]{:S(2)}, u32[]{:S(2)}) collective-permute-start(f32[64,128]{1,0:T(8,128)} %get-tuple-element.207), channel_id=1, source_target_pairs={{0,0},{1,2},{2,1},{3,4},{4,3},{5,6},{6,5},{7,8},{8,7},{9,10},{10,9... | collective-permute-start | bytes 98312 | tf_op jit(solution)/shard_map/ppermute | solution.py:287
  367.8 8.8 %collective-permute-start.45 = (f32[64,128]{1,0:T(8,128)}, f32[64,128]{1,0:T(8,128)S(1)}, u32[]{:S(2)}, u32[]{:S(2)}) collective-permute-start(f32[64,128]{1,0:T(8,128)} %get-tuple-element.217), channel_id=1, source_target_pairs={{0,0},{1,2},{2,1},{3,4},{4,3},{5,6},{6,5},{7,8},{8,7},{9,10},{10,9... | collective-permute-start | bytes 98312 | tf_op jit(solution)/shard_map/ppermute | solution.py:287
  389.5 9.4 %collective-permute-start.46 = (f32[64,128]{1,0:T(8,128)}, f32[64,128]{1,0:T(8,128)S(1)}, u32[]{:S(2)}, u32[]{:S(2)}) collective-permute-start(f32[64,128]{1,0:T(8,128)} %get-tuple-element.222), channel_id=1, source_target_pairs={{0,1},{1,0},{2,3},{3,2},{4,5},{5,4},{6,7},{7,6},{8,9},{9,8},{10,11... | collective-permute-start | bytes 98312 | tf_op jit(solution)/shard_map/ppermute | solution.py:287
  389.5 9.4 %collective-permute-start.47 = (f32[64,128]{1,0:T(8,128)}, f32[64,128]{1,0:T(8,128)S(1)}, u32[]{:S(2)}, u32[]{:S(2)}) collective-permute-start(f32[64,128]{1,0:T(8,128)} %get-tuple-element.223), channel_id=1, source_target_pairs={{0,0},{1,2},{2,1},{3,4},{4,3},{5,6},{6,5},{7,8},{8,7},{9,10},{10,9... | collective-permute-start | bytes 98312 | tf_op jit(solution)/shard_map/ppermute | solution.py:287
  394.6 17.3 %collective-permute-start.52 = (f32[64,128]{1,0:T(8,128)S(1)}, f32[64,128]{1,0:T(8,128)S(1)}, u32[]{:S(2)}, u32[]{:S(2)}) collective-permute-start(f32[64,128]{1,0:T(8,128)S(1)} %copy-done.74), channel_id=1, source_target_pairs={{0,1},{1,0},{2,3},{3,2},{4,5},{5,4},{6,7},{7,6},{8,9},{9,8},{10,11... | collective-permute-start | bytes 98312 | tf_op jit(solution)/shard_map/ppermute | solution.py:287
  394.9 17.0 %collective-permute-start.53 = (f32[64,128]{1,0:T(8,128)S(1)}, f32[64,128]{1,0:T(8,128)S(1)}, u32[]{:S(2)}, u32[]{:S(2)}) collective-permute-start(f32[64,128]{1,0:T(8,128)S(1)} %copy-done.73), channel_id=1, source_target_pairs={{0,0},{1,2},{2,1},{3,4},{4,3},{5,6},{6,5},{7,8},{8,7},{9,10},{10,9... | collective-permute-start | bytes 98312 | tf_op jit(solution)/shard_map/ppermute | solution.py:287
  405.7 11.9 %collective-permute-start.48 = (f32[64,128]{1,0:T(8,128)}, f32[64,128]{1,0:T(8,128)S(1)}, u32[]{:S(2)}, u32[]{:S(2)}) collective-permute-start(f32[64,128]{1,0:T(8,128)} %get-tuple-element.228), channel_id=1, source_target_pairs={{0,1},{1,0},{2,3},{3,2},{4,5},{5,4},{6,7},{7,6},{8,9},{9,8},{10,11... | collective-permute-start | bytes 98312 | tf_op jit(solution)/shard_map/ppermute | solution.py:287
  405.7 11.9 %collective-permute-start.49 = (f32[64,128]{1,0:T(8,128)}, f32[64,128]{1,0:T(8,128)S(1)}, u32[]{:S(2)}, u32[]{:S(2)}) collective-permute-start(f32[64,128]{1,0:T(8,128)} %get-tuple-element.229), channel_id=1, source_target_pairs={{0,0},{1,2},{2,1},{3,4},{4,3},{5,6},{6,5},{7,8},{8,7},{9,10},{10,9... | collective-permute-start | bytes 98312 | tf_op jit(solution)/shard_map/ppermute | solution.py:287
  (97 other events, 639.3 us)
